TPU v7x, 256 devices: a whole 4x4x8 slice. The times are simulated.
256 devices in a mesh: rep: 8 (over z), region: 32 (over y, x, core).
Axes of the slice: x: 4, y: 4, z: 8, core: 2. Of those that a mesh axis runs over, the one named last changes fastest.
Arguments:
- anchor: float32 [3, 32768], P(None, ('rep', 'region')), may hold values from -4 to 4
- direction: float32 [3, 32768], P(None, ('rep', 'region')), may hold values from -4 to 4
- seg_start: float32 [4, 32768], P(None, ('rep', 'region')), may hold values from 0 to 4
- seg_step: bfloat16 [4, 32768], P(None, ('rep', 'region')), may hold values from 0.019897461 to 0.119628906
- counts: int32 [4, 32768], P(None, ('rep', 'region')), may hold values from 1 to 16
- routes: int32 [32768, 4], P(('rep', 'region')), may hold values from 0 to 127, all different within a row; in each aligned block of 128 rows (0 to 127, 128 to 255, ...) at most 8 rows name the same one
- order: int32 [32768, 4], P(('rep', 'region')), may hold values from 0 to 3, each once within a row
- target: float32 [3, 32768], P(None, ('rep', 'region')), may hold values from 0 to 1
- fourier: float32 [3, 64], replicated, may hold values from -4 to 4
- w_input: bfloat16 [128, 128, 256], P('region'), may hold values from -0.5 to 0.5
- b_input: float32 [128, 256], P('region'), may hold values from -3 to 3
- w_middle: bfloat16 [128, 256, 256], P('region'), may hold values from -0.375 to 0.375
- b_middle: float32 [128, 256], P('region'), may hold values from -3 to 3
- w_output: bfloat16 [128, 4, 256], P('region'), may hold values from -0.375 to 0.375
Outputs:
- rendered: float32 [3, 32768], P(None, ('rep', 'region'))
- grad_w_input: float32 [128, 128, 256], P('region')
- grad_b_input: float32 [128, 256], P('region')
- grad_w_middle: float32 [128, 256, 256], P('region')
- grad_b_middle: float32 [128, 256], P('region')
- grad_w_output: float32 [128, 4, 256], P('region')
Inputs may be any that keep to these rules, and one draw needn't show every extreme that they name: `routes`: each ray names 4 different regions; among the rays of one device no region is named more than 8 times, and in every draw some region is named exactly 8 times by the rays of some device. `order`: each row is an ordering of 0 to 3.
All inputs are finite; a program needn't handle non-finite values.
Results may differ from a plain program's by a relative error of at most 0.004.
Values may be sent and summed in bfloat16 or wider, within the bound.
No kernel may reach another device: no remote copies, remote signals or barrier semaphores. Data moves between devices by JAX's collectives and lax.ppermute only.
A program may use at most 192 MiB of HBM per device.

v0:
```python
import functools
import math

import jax
import jax.numpy as jnp
import numpy as np
from jax import lax
from jax.experimental import pallas as pl
from jax.experimental.pallas import tpu as pltpu
from jax.sharding import PartitionSpec as P

SEG = 16
CH = 64
F32, BF16 = jnp.float32, jnp.bfloat16
VM = pltpu.VMEM
NT = (((1,), (1,)), ((), ()))
TN = (((0,), (0,)), ((), ()))


def _sine_coeffs():
    k = np.arange(64)
    y = 0.125 + 0.125 * np.cos(math.pi * (k + 0.5) / 64)
    r = np.sqrt(y)
    poly = np.polynomial.chebyshev.Chebyshev.interpolate(
        lambda q: np.sin(2 * math.pi * np.sqrt(q)) / np.sqrt(q), 5, domain=[1e-12, 0.25]
    )
    return [float(c) for c in poly.convert(kind=np.polynomial.Polynomial).coef]


COEF = _sine_coeffs()


def sine_turns(u):
    r = u - jnp.round(u)
    y = r * r
    p = jnp.full_like(y, COEF[5])
    for c in COEF[4::-1]:
        p = p * y + c
    return p * r


def split3(x):
    hi = x.astype(BF16)
    rest = x - hi.astype(F32)
    mid = rest.astype(BF16)
    low = (rest - mid.astype(F32)).astype(BF16)
    return hi, mid, low


def pick(a, b, dims, split_first):
    if split_first:
        parts = [lax.dot_general(x, b, dims, preferred_element_type=F32) for x in split3(a)]
    else:
        parts = [lax.dot_general(a, x, dims, preferred_element_type=F32) for x in split3(b)]
    return (parts[0] + parts[1]) + parts[2]


def iota(shape, dim):
    return lax.broadcasted_iota(jnp.int32, shape, dim)


def dispatch(slot, vals, groups):
    entries = slot.shape[1]
    dest = (iota((groups, entries), 0) == slot // 32).astype(F32).astype(BF16)
    lane = iota((32, entries), 0) == slot % 32
    rows = jnp.concatenate([jnp.where(lane, v, 0.0) for v in vals], axis=0)
    return pick(dest, rows, NT, False)


def send_kernel(anchor, direction, start, step, counts, routes, geo_out, slot_out):
    groups = geo_out.shape[0]
    regs = jnp.concatenate([routes[k : k + 1, :] for k in range(4)], axis=1)
    entries = regs.shape[1]
    regions = groups * 4
    hot = (iota((regions, entries), 0) == regs).astype(F32)
    upper = (iota((entries, entries), 0) < iota((entries, entries), 1)).astype(F32).astype(BF16)
    earlier = jnp.dot(hot.astype(BF16), upper, preferred_element_type=F32)
    rank = jnp.sum(hot * earlier, axis=0, keepdims=True).astype(jnp.int32)
    slot = regs * 8 + rank
    slot_out[...] = slot
    stp = step[...].astype(F32)
    cnt = counts[...].astype(F32)
    rows = []
    for c in range(3):
        rows.append(
            jnp.concatenate(
                [anchor[c : c + 1, :] + start[k : k + 1, :] * direction[c : c + 1, :] for k in range(4)],
                axis=1,
            )
        )
    rows.append(jnp.concatenate([cnt[k : k + 1, :] for k in range(4)], axis=1))
    for c in range(3):
        rows.append(
            jnp.concatenate([stp[k : k + 1, :] * direction[c : c + 1, :] for k in range(4)], axis=1)
        )
    rows.append(jnp.concatenate([stp[k : k + 1, :] for k in range(4)], axis=1))
    geo_out[:, 0, :] = dispatch(slot, rows[:4], groups)
    geo_out[:, 1, :] = dispatch(slot, rows[4:], groups)


def region_plan(geo0, s):
    groups = geo0.shape[0]
    lanes = iota((groups, 128), 1)
    live = jnp.where((lanes // 8 == 12 + s) & (geo0 > 0.5), 1.0, 0.0)
    num = jnp.sum(live, axis=1, keepdims=True)
    before = iota((groups, groups), 1) < iota((groups, groups), 0)
    first = jnp.dot(
        before.astype(F32).astype(BF16),
        jnp.broadcast_to(num, (groups, 128)).astype(BF16),
        preferred_element_type=F32,
    )[:, :1]
    return num, first


def chunk_map(num, first, base):
    groups = num.shape[0]
    j = (iota((groups, 128), 1) % CH + base).astype(F32)
    src = jnp.where((j >= first) & (j < first + num), 1.0, 0.0)
    place = (j[:1, :] - jnp.sum(src * first, axis=0, keepdims=True)).astype(jnp.int32)
    return src.astype(BF16), place


def chunk_take(arr, src, place, s):
    full = pick(arr, src, TN, True)
    mask = iota((8, 128), 0) == place
    rows = []
    for w in range(4):
        part = jnp.zeros((8, 128), F32)
        for t in range(4):
            at = w * 32 + t * 8
            part = jnp.where(s == t, full[at : at + 8, :], part)
        rows.append(jnp.sum(jnp.where(mask, part, 0.0), axis=0, keepdims=True))
    return rows


def encode(head, rest, fcol):
    px, py, pz, count = head
    dx, dy, dz, step = rest
    fx, fy, fz, turn = (fcol[:, c : c + 1] for c in range(4))
    begin = px * fx + py * fy + pz * fz
    slope = dx * fx + dy * fy + dz * fz
    half = (iota((1, 128), 1) // CH).astype(F32)
    begin = begin + (half + 0.5) * slope + turn
    begin = (begin - jnp.round(begin)).T
    slope = (slope - jnp.round(slope)).T
    feats = [sine_turns(begin + (2.0 * p) * slope).astype(BF16) for p in range(8)]
    return jnp.concatenate(feats, axis=0)


def sigmoid(v):
    return 0.5 * jnp.tanh(0.5 * v) + 0.5


def layers(feat, w_in, b_in, w_mid, b_mid):
    z1 = jnp.dot(feat, w_in, preferred_element_type=F32) + b_in
    s1 = sigmoid(z1)
    h1 = z1 * s1
    h1b = h1.astype(BF16)
    z2 = jnp.dot(h1b, w_mid, preferred_element_type=F32) + b_mid
    s2 = sigmoid(z2)
    h2 = z2 * s2
    return s1, h1, h1b, s2, h2, h2.astype(BF16)


def both(row):
    return row + pltpu.roll(row, CH, 1)


def segment_terms(head_t, count, step):
    upper_half = iota((1, 128), 1) >= CH
    half = (iota((1, 128), 1) // CH).astype(F32)
    total = jnp.zeros((1, 128), F32)
    terms = []
    for p in range(8):
        blk = head_t[:, p * 128 : (p + 1) * 128]
        spacing = jnp.where(2.0 * p + half < count, step, 0.0)
        top = blk[:1, :]
        density = jnp.maximum(top, 0.0) + jnp.log1p(jnp.exp(-jnp.abs(top)))
        optical = density * spacing
        other = pltpu.roll(optical, CH, 1)
        before = total + jnp.where(upper_half, other, 0.0)
        total = total + optical + other
        reach = jnp.exp(-before)
        keep = jnp.exp(-optical)
        terms.append((spacing, reach, keep, reach * (1.0 - keep), sigmoid(blk)))
    return terms, jnp.exp(-total)


def forward_kernel(geo, fcol, w_in, b_in, w_mid, b_mid, w_head, res_out):
    s = pl.program_id(0)
    geo0, geo1 = geo[:, 0, :], geo[:, 1, :]
    groups = geo0.shape[0]
    num, first = region_plan(geo0, s)
    amount = jnp.sum(num).astype(jnp.int32)

    @pl.when(s == 0)
    def _():
        res_out[...] = jnp.zeros_like(res_out)

    def step_of(i, carry):
        src, place = chunk_map(num, first, i * CH)
        head = chunk_take(geo0, src, place, s)
        rest = chunk_take(geo1, src, place, s)
        feat = encode(head, rest, fcol)
        h2b = layers(feat, w_in[0], b_in[0], w_mid[0], b_mid[0])[5]
        head_t = lax.dot_general(w_head[0], h2b, NT, preferred_element_type=F32)[:8]
        terms, passed = segment_terms(head_t, head[3], rest[3])
        colour = jnp.zeros((8, 128), F32)
        for _, _, _, share, tint in terms:
            colour = colour + share * tint
        colour = both(colour)
        first_half = iota((1, 128), 1) < CH
        mask = (iota((8, 128), 0) == place) & first_half
        blocks = []
        for w in range(4):
            row = passed if w == 3 else colour[w + 1 : w + 2, :]
            hit = jnp.where(mask, row, 0.0)
            for t in range(4):
                blocks.append(jnp.where(s == t, hit, 0.0))
        z = jnp.concatenate(blocks, axis=0)
        res_out[...] += pick(src, z, NT, False)
        return carry

    lax.fori_loop(0, (amount + CH - 1) // CH, step_of, 0)


def merge_kernel(slot, order, target, res, rendered_out, cot_out):
    groups = res.shape[0]
    sl = slot[...]
    entries = sl.shape[1]
    dest = (iota((groups, entries), 0) == sl // 32).astype(F32).astype(BF16)
    full = pick(res[...], dest, TN, True)
    lane = iota((32, entries), 0) == sl % 32
    vals = [
        jnp.sum(jnp.where(lane, full[w * 32 : (w + 1) * 32, :], 0.0), axis=0, keepdims=True)
        for w in range(4)
    ]
    rays = entries // 4
    seg = [[vals[w][:, k * rays : (k + 1) * rays] for w in range(4)] for k in range(4)]
    which = [order[j : j + 1, :] for j in range(4)]
    ordered = []
    for j in range(4):
        ordered.append(
            [sum(jnp.where(which[j] == k, seg[k][w], 0.0) for k in range(4)) for w in range(4)]
        )
    carried = [jnp.ones((1, rays), F32)]
    colour = [jnp.zeros((1, rays), F32)] * 3
    for j in range(4):
        colour = [colour[c] + carried[j] * ordered[j][c] for c in range(3)]
        carried.append(carried[j] * ordered[j][3])
    for c in range(3):
        rendered_out[c : c + 1, :] = colour[c]
    grad = [(colour[c] - target[c : c + 1, :]) * (1.0 / 16.0) for c in range(3)]
    cots = [None] * 4
    tail = jnp.zeros((1, rays), F32)
    for j in (3, 2, 1, 0):
        cots[j] = [carried[j] * g for g in grad] + [carried[j] * tail]
        tail = sum(ordered[j][c] * grad[c] for c in range(3)) + ordered[j][3] * tail
    rows = []
    for w in range(4):
        rows.append(
            jnp.concatenate(
                [sum(jnp.where(which[j] == k, cots[j][w], 0.0) for j in range(4)) for k in range(4)],
                axis=1,
            )
        )
    cot_out[...] = dispatch(sl, rows, groups)


def backward_kernel(geo, cot, fcol, w_in, b_in, w_mid, b_mid, w_head, out, g_in, g_mid, g_bin, g_bmid, g_head):
    s = pl.program_id(0)
    geo0, geo1 = geo[:, 0, :], geo[:, 1, :]
    num, first = region_plan(geo0, s)
    amount = jnp.sum(num).astype(jnp.int32)
    for ref in (g_in, g_mid, g_bin, g_bmid, g_head):
        ref[...] = jnp.zeros_like(ref)

    def step_of(i, carry):
        src, place = chunk_map(num, first, i * CH)
        head = chunk_take(geo0, src, place, s)
        rest = chunk_take(geo1, src, place, s)
        given = chunk_take(cot[...], src, place, s)
        feat = encode(head, rest, fcol)
        s1, h1, h1b, s2, h2, h2b = layers(feat, w_in[0], b_in[0], w_mid[0], b_mid[0])
        head_t = lax.dot_general(w_head[0], h2b, NT, preferred_element_type=F32)[:8]
        terms, passed = segment_terms(head_t, head[3], rest[3])
        zero = jnp.zeros((1, 128), F32)
        paint = jnp.concatenate([zero, given[0], given[1], given[2], zero, zero, zero, zero], axis=0)
        lower_half = iota((1, 128), 1) < CH
        after = given[3] * passed
        top_row = iota((8, 128), 0) == 0
        cots = [None] * 8
        for p in range(7, -1, -1):
            spacing, reach, keep, share, tint = terms[p]
            weight = jnp.sum(paint * tint, axis=0, keepdims=True)
            gain = share * weight
            other = pltpu.roll(gain, CH, 1)
            later = after + jnp.where(lower_half, other, 0.0)
            after = after + gain + other
            g_opt = (reach * keep * weight - later) * spacing
            cots[p] = jnp.where(top_row, g_opt * tint, paint * share * tint * (1.0 - tint))
        cot_t = jnp.concatenate(cots, axis=1)
        cot_t = jnp.concatenate([cot_t, jnp.zeros_like(cot_t)], axis=0)
        cot_b = cot_t.astype(BF16)
        g_head[...] += jnp.dot(cot_b, h2b, preferred_element_type=F32)
        gh2 = lax.dot_general(cot_b, w_head[0], TN, preferred_element_type=F32)
        gz2 = gh2 * (s2 + h2 * (1.0 - s2))
        gz2b = gz2.astype(BF16)
        g_mid[...] += lax.dot_general(h1b, gz2b, TN, preferred_element_type=F32)
        g_bmid[...] += jnp.sum(gz2.reshape(-1, 8, gz2.shape[1]), axis=0)
        gh1 = lax.dot_general(gz2b, w_mid[0], NT, preferred_element_type=F32)
        gz1 = gh1 * (s1 + h1 * (1.0 - s1))
        gz1b = gz1.astype(BF16)
        g_in[...] += lax.dot_general(feat, gz1b, TN, preferred_element_type=F32)
        g_bin[...] += jnp.sum(gz1.reshape(-1, 8, gz1.shape[1]), axis=0)
        return carry

    lax.fori_loop(0, (amount + CH - 1) // CH, step_of, 0)
    enc = g_in.shape[0]
    hid = g_mid.shape[0]
    out[0, 0:enc, :] = g_in[...].astype(BF16)
    out[0, enc : enc + hid, :] = g_mid[...].astype(BF16)
    row = iota(g_head.shape, 0)
    b1 = jnp.sum(g_bin[...], axis=0, keepdims=True)
    b2 = jnp.sum(g_bmid[...], axis=0, keepdims=True)
    tail = jnp.where(row == 8, b1, jnp.where(row == 9, b2, g_head[...]))
    out[0, enc + hid : enc + hid + 16, :] = tail.astype(BF16)
    out[0, enc + hid + 16 : enc + hid + 32, :] = jnp.zeros_like(tail).astype(BF16)


def total_kernel(parts, out):
    acc = parts[0].astype(F32)
    for i in range(1, parts.shape[0]):
        acc = acc + parts[i].astype(F32)
    out[...] = acc.astype(BF16)


def spread_kernel(packed, o_in, o_bin, o_mid, o_bmid, o_head):
    regions, enc, hid = o_in.shape
    for s in range(regions):
        o_in[s] = packed[s, 0:enc, :].astype(F32)
        o_mid[s] = packed[s, enc : enc + hid, :].astype(F32)
        tail = packed[s, enc + hid : enc + hid + 16, :].astype(F32)
        o_head[s] = tail[0:4, :]
        o_bin[s : s + 1, :] = tail[8:9, :]
        o_bmid[s : s + 1, :] = tail[9:10, :]


def call(kernel, outs, *args, **more):
    return pl.pallas_call(
        kernel,
        out_shape=outs,
        compiler_params=pltpu.CompilerParams(vmem_limit_bytes=56 * 2**20),
        **more,
    )(*args)


def struct(*shape, dtype=F32):
    return jax.ShapeDtypeStruct(shape, dtype)


def a2a(x, axis):
    return lax.all_to_all(x, axis, split_axis=0, concat_axis=0, tiled=True)


def body(
    anchor, direction, seg_start, seg_step, counts, routes, order, target,
    fourier, w_input, b_input, w_middle, b_middle, w_output,
):
    groups = lax.axis_size("region")
    reps = lax.axis_size("rep")
    subs, enc, hid = w_input.shape
    rays = anchor.shape[1]
    freqs = fourier.shape[1]
    fcol = jnp.zeros((enc, 128), F32)
    fcol = fcol.at[:, 0:3].set(jnp.concatenate([fourier.T, fourier.T], axis=0))
    fcol = fcol.at[freqs:, 3].set(0.25)
    w_head = jnp.pad(w_output, ((0, 0), (0, 12), (0, 0)))
    b_in, b_mid = b_input[:, None, :], b_middle[:, None, :]

    geo_send, slot = call(
        send_kernel,
        (struct(groups, 2, 128), struct(1, rays * 4, dtype=jnp.int32)),
        anchor, direction, seg_start, seg_step, counts, routes.T,
    )
    geo = a2a(geo_send, "region")

    def whole(*shape):
        return pl.BlockSpec(shape, lambda s: (0,) * len(shape))

    def per_region(*shape):
        return pl.BlockSpec((1,) + shape, lambda s: (s,) + (0,) * len(shape))

    net_specs = [
        whole(enc, 128), per_region(enc, hid), per_region(1, hid), per_region(hid, hid),
        per_region(1, hid), per_region(16, hid),
    ]
    net = (fcol, w_input, b_in, w_middle, b_mid, w_head)
    res = call(
        forward_kernel,
        struct(groups, 128),
        geo, *net,
        grid=(subs,),
        in_specs=[whole(groups, 2, 128)] + net_specs,
        out_specs=whole(groups, 128),
    )
    res_back = a2a(res[:, None, :], "region")[:, 0, :]
    rendered, cot_send = call(
        merge_kernel,
        (struct(3, rays), struct(groups, 128)),
        slot, order.T, target, res_back,
    )
    cot = a2a(cot_send[:, None, :], "region")[:, 0, :]
    rows = enc + hid + 32
    packed = call(
        backward_kernel,
        struct(subs, rows, hid, dtype=BF16),
        geo, cot, *net,
        grid=(subs,),
        in_specs=[whole(groups, 2, 128), whole(groups, 128)] + net_specs,
        out_specs=per_region(rows, hid),
        scratch_shapes=[
            VM((enc, hid), F32), VM((hid, hid), F32), VM((8, hid), F32), VM((8, hid), F32), VM((16, hid), F32),
        ],
    )
    parts = a2a(packed.reshape(reps, subs * rows // reps, hid), "rep")
    mine = call(total_kernel, struct(subs * rows // reps, hid, dtype=BF16), parts)
    full = lax.all_gather(mine, "rep", axis=0, tiled=True).reshape(subs, rows, hid)
    grads = call(
        spread_kernel,
        (struct(subs, enc, hid), struct(subs, hid), struct(subs, hid, hid), struct(subs, hid), struct(subs, 4, hid)),
        full,
    )
    return (rendered, *grads)


def solution(mesh):
    rays, own = ("rep", "region"), "region"
    return jax.shard_map(
        body,
        mesh=mesh,
        in_specs=(
            P(None, rays), P(None, rays), P(None, rays), P(None, rays), P(None, rays),
            P(rays, None), P(rays, None), P(None, rays), P(),
            P(own, None, None), P(own, None), P(own, None, None), P(own, None), P(own, None, None),
        ),
        out_specs=(
            P(None, rays), P(own, None, None), P(own, None), P(own, None, None), P(own, None), P(own, None, None),
        ),
        check_vma=False,
    )
```

profile of v0, /device:TPU:2, one launch (start us, length us, event | category | flops | bytes accessed | tf_op | source)
XLA Modules:
  0.0 164.1 jit_solution(10409132993234177362)
XLA Ops:
  0.6 2.0 %shard_map.181 = (f32[32,2,128]{2,1,0:T(2,128)}, s32[1,512]{1,0:T(1,128)}) custom-call(f32[3,128]{1,0:T(4,128)} %anchor.1, f32[3,128]{1,0:T(4,128)} %direction.1, f32[4,128]{1,0:T(4,128)} %start.1, bf16[4,128]{1,0:T(4,128)(2,1)} %step.1, s32[4,128]{1,0:T(4,128)} %counts.1, s32[4,128]{1,0:T(4,128)} %bitcast.20), custom_call_target="tpu_custom_call" | custom-call | tf_op jit(solution)/shard_map/pallas_call | solution.py:350
  2.7 7.6 %all-to-all-start = ((f32[32,2,128]{2,1,0:T(2,128)}), f32[32,2,128]{2,1,0:T(2,128)S(1)}, u32[]{:S(2)}, u32[]{:S(2)}) async-start(f32[32,2,128]{2,1,0:T(2,128)} %get-tuple-element.40), calls=%async_computation | async-start | bytes 65536 | tf_op jit(solution)/shard_map/all_to_all | solution.py:363
  10.3 0.0 copy-start.5
  10.3 0.6 compare_reduce_fusion
  11.0 0.0 copy-done.5
  11.0 0.1 pad_maximum_fusion
  11.1 0.1 copy.21
  11.2 0.0 copy-start.3
  11.2 0.0 copy-start.4
  11.2 0.7 broadcast_select_fusion
  11.9 0.0 copy-done.3
  11.9 0.0 copy-start.2
  11.9 0.6 broadcast_in_dim.14.b_in
  12.5 0.0 copy-done.4
  12.5 0.6 broadcast_in_dim.15.b_mid
  13.1 0.0 copy-done.2
  13.1 0.6 pad.10.w_head
  13.7 0.5 scatter.9.fcol
  14.3 0.0 copy-start
  14.3 2.2 %all-to-all-done.geo = f32[32,2,128]{2,1,0:T(2,128)S(1)} async-done(((f32[32,2,128]{2,1,0:T(2,128)}), f32[32,2,128]{2,1,0:T(2,128)S(1)}, u32[]{:S(2)}, u32[]{:S(2)}) %all-to-all-start) | async-done | bytes 32800 | tf_op jit(solution)/shard_map/all_to_all | solution.py:363
  16.5 0.0 copy-done
  16.5 0.0 copy-start.1
  16.5 0.6 copy-done.1
  17.1 25.1 %shard_map.182 = f32[32,128]{1,0:T(8,128)} custom-call(f32[32,2,128]{2,1,0:T(2,128)} %copy-done.1, f32[128,128]{1,0:T(8,128)} %copy-done, bf16[4,128,256]{2,1,0:T(8,128)(2,1)} %w_in.3, f32[4,1,256]{2,1,0:T(1,128)} %broadcast_in_dim.14.b_in, bf16[4,256,256]{2,1,0:T(8,128)(2,1)} %w_mid.3, f32[4,1,256]{2,1,0:T(1,128)} %broadcast_in_dim.15.b_mid, ...), custom_call_target="tpu_custom_call" | custom-call | tf_op jit(solution)/shard_map/pallas_call | solution.py:350
  42.2 10.1 %all_to_all.20 = f32[32,1,128]{2,1,0:T(1,128)} all-to-all(f32[32,1,128]{2,1,0:T(1,128)} %bitcast.16), channel_id=1, replica_groups=mesh['rep'=8,'region'=32] {'region'}, dimensions={0} | all-to-all | bytes 32768 | tf_op jit(solution)/shard_map/all_to_all | solution.py:363
  52.3 2.1 %shard_map.183 = (f32[3,128]{1,0:T(4,128)}, f32[32,128]{1,0:T(8,128)}) custom-call(s32[1,512]{1,0:T(1,128)} %get-tuple-element.39.slot, s32[4,128]{1,0:T(4,128)} %bitcast.21, f32[3,128]{1,0:T(4,128)} %target.1, f32[32,128]{1,0:T(8,128)} %bitcast.17), custom_call_target="tpu_custom_call" | custom-call | tf_op jit(solution)/shard_map/pallas_call | solution.py:350
  54.4 11.7 %all_to_all.21 = f32[32,1,128]{2,1,0:T(1,128)} all-to-all(f32[32,1,128]{2,1,0:T(1,128)} %bitcast.18), channel_id=1, replica_groups=mesh['rep'=8,'region'=32] {'region'}, dimensions={0} | all-to-all | bytes 32768 | tf_op jit(solution)/shard_map/all_to_all | solution.py:363
  66.1 34.1 %shard_map.184 = bf16[4,416,256]{2,1,0:T(8,128)(2,1)} custom-call(f32[32,2,128]{2,1,0:T(2,128)} %copy-done.1, f32[32,128]{1,0:T(8,128)} %bitcast.15, f32[128,128]{1,0:T(8,128)} %copy-done, bf16[4,128,256]{2,1,0:T(8,128)(2,1)} %w_in.3, f32[4,1,256]{2,1,0:T(1,128)} %broadcast_in_dim.14.b_in, bf16[4,256,256]{2,1,0:T(8,128)(2,1)} %w_mid.3, ...), custom_call_target="tpu_custom_call" | custom-call | tf_op jit(solution)/shard_map/pallas_call | solution.py:350
  100.3 30.9 %all_to_all.22.parts = bf16[8,208,256]{2,1,0:T(8,128)(2,1)} all-to-all(bf16[8,208,256]{2,1,0:T(8,128)(2,1)} %bitcast.13), channel_id=1, replica_groups=mesh['rep'=8,'region'=32] {'rep'}, dimensions={0} | all-to-all | bytes 1703936 | tf_op jit(solution)/shard_map/all_to_all | solution.py:363
  131.2 1.9 %shard_map.185 = bf16[208,256]{1,0:T(8,128)(2,1)} custom-call(bf16[8,208,256]{2,1,0:T(8,128)(2,1)} %all_to_all.22.parts), custom_call_target="tpu_custom_call" | custom-call | tf_op jit(solution)/shard_map/pallas_call | solution.py:350
  133.1 28.6 %all_gather.3 = bf16[1664,256]{1,0:T(8,128)(2,1)} all-gather(bf16[208,256]{1,0:T(8,128)(2,1)} %shard_map.185), channel_id=1, replica_groups=mesh['rep'=8,'region'=32] {'rep'}, dimensions={0}, use_global_device_ids=true | all-gather | bytes 958464 | tf_op jit(solution)/shard_map/all_gather | solution.py:428
  161.7 2.4 %shard_map.186 = (f32[4,128,256]{2,1,0:T(8,128)}, f32[4,256]{1,0:T(4,128)}, f32[4,256,256]{2,1,0:T(8,128)}, f32[4,256]{1,0:T(4,128)}, f32[4,4,256]{2,1,0:T(4,128)}) custom-call(bf16[4,416,256]{2,1,0:T(8,128)(2,1)} %bitcast.14), custom_call_target="tpu_custom_call" | custom-call | tf_op jit(solution)/shard_map/pallas_call | solution.py:350
  (2 shorter events, 0.0 us)
Async XLA Ops:
  2.7 13.8 %all-to-all-start = ((f32[32,2,128]{2,1,0:T(2,128)}), f32[32,2,128]{2,1,0:T(2,128)S(1)}, u32[]{:S(2)}, u32[]{:S(2)}) async-start(f32[32,2,128]{2,1,0:T(2,128)} %get-tuple-element.40), calls=%async_computation | async-start | bytes 65536 | tf_op jit(solution)/shard_map/all_to_all | solution.py:363
  10.3 0.7 copy-start.5
  11.2 0.7 copy-start.3
  11.2 1.3 copy-start.4
  11.9 1.2 copy-start.2
  14.3 2.3 %copy-start = (f32[128,128]{1,0:T(8,128)}, f32[128,128]{1,0:T(8,128)S(1)}, u32[]{:S(2)}) copy-start(f32[128,128]{1,0:T(8,128)S(1)} %scatter.9.fcol) | copy-start | bytes 196612
  16.5 0.6 copy-start.1
where the time goes:
time: 165 us; the launch traced here: 164 us
  blocking collectives  81.3 us (49%)
  Pallas kernels  67.6 us (41%)
  starting transfers between devices  7.62 us (5%)
  local copies, waits for them, and re-layouts  3.12 us (2%)
  waiting for transfers between devices  2.24 us (1%)
    pallas_call x6, Pallas kernels, call(): pl.pallas_call(kernel, out_shape=outs, compiler_params=pltpu.CompilerPara...  67.6 us
    all_to_all x3, blocking collectives, a2a(): return lax.all_to_all(x, axis, split_axis=0, concat_axis=0, tiled=True)  52.7 us
    all_gather x1, blocking collectives, body(): lax.all_gather(mine, 'rep', axis=0, tiled=True).reshape(subs, rows, hid)  28.6 us
    all_to_all x1, starting transfers between devices, a2a(): return lax.all_to_all(x, axis, split_axis=0, concat_axis=0, tiled=True)  7.62 us
  transfers between devices with their start and end apart: 1, of which 1 were waited for; matrix products, arithmetic and copies ran while one was open for 2% of the time, Pallas kernels for 0%

commit v1 on v0

--- a/solution.py
+++ b/solution.py
@@ -10,6 +10,7 @@
 from jax.sharding import PartitionSpec as P
 
 SEG = 16
+PAD = 32
 CH = 64
 F32, BF16 = jnp.float32, jnp.bfloat16
 VM = pltpu.VMEM
@@ -112,25 +113,31 @@
     return num, first
 
 
-def chunk_map(num, first, base):
+def region_map(num, first):
     groups = num.shape[0]
-    j = (iota((groups, 128), 1) % CH + base).astype(F32)
+    wide = groups * 8 * 2
+    lane = iota((groups, wide), 1)
+    j = (lane // 128 * CH + lane % CH).astype(F32)
     src = jnp.where((j >= first) & (j < first + num), 1.0, 0.0)
     place = (j[:1, :] - jnp.sum(src * first, axis=0, keepdims=True)).astype(jnp.int32)
     return src.astype(BF16), place
 
 
-def chunk_take(arr, src, place, s):
+def region_take(arr, src, place, s):
     full = pick(arr, src, TN, True)
-    mask = iota((8, 128), 0) == place
-    rows = []
-    for w in range(4):
-        part = jnp.zeros((8, 128), F32)
-        for t in range(4):
-            at = w * 32 + t * 8
-            part = jnp.where(s == t, full[at : at + 8, :], part)
-        rows.append(jnp.sum(jnp.where(mask, part, 0.0), axis=0, keepdims=True))
-    return rows
+    mask = iota((8, src.shape[1]), 0) == place
+    return [
+        jnp.sum(jnp.where(mask, full[w * 32 + s * 8 : w * 32 + s * 8 + 8, :], 0.0), axis=0, keepdims=True)
+        for w in range(4)
+    ]
+
+
+def find(n, ends):
+    s = sum((n >= e).astype(jnp.int32) for e in ends[:-1])
+    start = jnp.int32(0)
+    for e in ends[:-1]:
+        start = jnp.where(n >= e, e, start)
+    return s, n - start
 
 
 def encode(head, rest, fcol):
@@ -143,23 +150,35 @@
     begin = begin + (half + 0.5) * slope + turn
     begin = (begin - jnp.round(begin)).T
     slope = (slope - jnp.round(slope)).T
-    feats = [sine_turns(begin + (2.0 * p) * slope).astype(BF16) for p in range(8)]
+    slope = slope + slope
+    feats = []
+    for p in range(8):
+        feats.append(sine_turns(begin).astype(BF16))
+        begin = begin + slope
     return jnp.concatenate(feats, axis=0)
+
+
+def columns_of(fourier):
+    both_halves = jnp.concatenate([fourier, fourier], axis=1)
+    width = both_halves.shape[1]
+    turn = jnp.where(iota((1, width), 1) >= width // 2, 0.25, 0.0)
+    return jnp.concatenate([both_halves, turn, jnp.zeros((width - 4, width), F32)], axis=0).T
+
+
+def head_rows(w):
+    w = w.astype(F32)
+    return jnp.concatenate([w, jnp.zeros((12, w.shape[1]), F32)], axis=0)
 
 
 def sigmoid(v):
     return 0.5 * jnp.tanh(0.5 * v) + 0.5
 
 
-def layers(feat, w_in, b_in, w_mid, b_mid):
-    z1 = jnp.dot(feat, w_in, preferred_element_type=F32) + b_in
-    s1 = sigmoid(z1)
-    h1 = z1 * s1
-    h1b = h1.astype(BF16)
-    z2 = jnp.dot(h1b, w_mid, preferred_element_type=F32) + b_mid
-    s2 = sigmoid(z2)
-    h2 = z2 * s2
-    return s1, h1, h1b, s2, h2, h2.astype(BF16)
+def layer(x, w_half, b_half):
+    v = jnp.dot(x, w_half, preferred_element_type=F32) + b_half
+    t = jnp.tanh(v)
+    q = v * t
+    return (v + q).astype(BF16), ((1.0 + t) * ((1.0 + v) - q)).astype(BF16)
 
 
 def both(row):
@@ -186,42 +205,88 @@
     return terms, jnp.exp(-total)
 
 
-def forward_kernel(geo, fcol, w_in, b_in, w_mid, b_mid, w_head, res_out):
-    s = pl.program_id(0)
+def forward_kernel(
+    geo, fourier, w_in, b_in, w_mid, b_mid, w_head, res_out, rows_out, heads_out, chunks_out, kept_out,
+    seg_rows, w_in_half, w_mid_half, heads, kept, sem,
+):
+    fcol = columns_of(fourier[...])
     geo0, geo1 = geo[:, 0, :], geo[:, 1, :]
-    groups = geo0.shape[0]
-    num, first = region_plan(geo0, s)
-    amount = jnp.sum(num).astype(jnp.int32)
-
-    @pl.when(s == 0)
-    def _():
-        res_out[...] = jnp.zeros_like(res_out)
-
-    def step_of(i, carry):
-        src, place = chunk_map(num, first, i * CH)
-        head = chunk_take(geo0, src, place, s)
-        rest = chunk_take(geo1, src, place, s)
-        feat = encode(head, rest, fcol)
-        h2b = layers(feat, w_in[0], b_in[0], w_mid[0], b_mid[0])[5]
-        head_t = lax.dot_general(w_head[0], h2b, NT, preferred_element_type=F32)[:8]
-        terms, passed = segment_terms(head_t, head[3], rest[3])
+    enc, hid = w_in.shape[1:]
+    subs = w_in.shape[0]
+    maps, ends = [], []
+    total = jnp.int32(0)
+    for s in range(subs):
+        num, first = region_plan(geo0, s)
+        amount = (jnp.sum(num).astype(jnp.int32) + CH - 1) // CH
+        chunks_out[s] = amount
+        w_in_half[s] = w_in[s] * 0.5
+        w_mid_half[s] = w_mid[s] * 0.5
+        heads[s] = head_rows(w_head[s]).astype(BF16)
+        total = total + amount
+        ends.append(total)
+        src, place = region_map(num, first)
+        maps.append((src, place))
+        rows_out[s] = jnp.concatenate(
+            region_take(geo0, src, place, s) + region_take(geo1, src, place, s), axis=0
+        )
+    seg_rows[...] = jnp.zeros_like(seg_rows)
+    per = rows_out.shape[2] // 128
+
+    def copy(slot, at):
+        return pltpu.make_async_copy(kept.at[slot], kept_out.at[at], sem.at[slot])
+
+    def step_of(n, carry):
+        s, i = find(n, ends)
+        slot = n % 2
+
+        @pl.when(n >= 2)
+        def _():
+            copy(slot, 0).wait()
+
+        lanes = pl.ds(pl.multiple_of(i * 128, 128), 128)
+        rows = rows_out[s, :, lanes]
+        rows = [rows[w : w + 1, :] for w in range(8)]
+        feat = encode(rows[:4], rows[4:], fcol)
+        h1b, slope1 = layer(feat, w_in_half[s], b_in[pl.ds(s, 1), :] * 0.5)
+        h2b, slope2 = layer(h1b, w_mid_half[s], b_mid[pl.ds(s, 1), :] * 0.5)
+        at = 0
+        for part in (feat, h1b, h2b, slope1, slope2):
+            kept[slot, :, at : at + part.shape[1]] = part
+            at += part.shape[1]
+        copy(slot, s * per + i).start()
+        head_t = lax.dot_general(heads[s], h2b, NT, preferred_element_type=F32)[:8]
+        heads_out[s * per + i] = head_t
+        terms, passed = segment_terms(head_t, rows[3], rows[7])
         colour = jnp.zeros((8, 128), F32)
         for _, _, _, share, tint in terms:
             colour = colour + share * tint
         colour = both(colour)
-        first_half = iota((1, 128), 1) < CH
-        mask = (iota((8, 128), 0) == place) & first_half
+        seg_rows[s, :, lanes] = jnp.where(iota((8, 128), 0) == 0, passed, colour)
+        return carry
+
+    lax.fori_loop(0, total, step_of, 0)
+
+    @pl.when(total >= 1)
+    def _():
+        copy((total - 1) % 2, 0).wait()
+
+    @pl.when(total >= 2)
+    def _():
+        copy(total % 2, 0).wait()
+
+    acc = jnp.zeros(res_out.shape, F32)
+    for s in range(subs):
+        src, place = maps[s]
+        wide = src.shape[1]
+        mask = (iota((8, wide), 0) == place) & (iota((8, wide), 1) % 128 < CH)
+        none = jnp.zeros((8, wide), F32)
         blocks = []
         for w in range(4):
-            row = passed if w == 3 else colour[w + 1 : w + 2, :]
-            hit = jnp.where(mask, row, 0.0)
-            for t in range(4):
-                blocks.append(jnp.where(s == t, hit, 0.0))
-        z = jnp.concatenate(blocks, axis=0)
-        res_out[...] += pick(src, z, NT, False)
-        return carry
-
-    lax.fori_loop(0, (amount + CH - 1) // CH, step_of, 0)
+            row = (w + 1) % 4
+            hit = jnp.where(mask, seg_rows[s, row : row + 1, :], 0.0)
+            blocks += [hit if t == s else none for t in range(4)]
+        acc = acc + pick(src, jnp.concatenate(blocks, axis=0), NT, False)
+    res_out[...] = acc
 
 
 def merge_kernel(slot, order, target, res, rendered_out, cot_out):
@@ -267,28 +332,58 @@
     cot_out[...] = dispatch(sl, rows, groups)
 
 
-def backward_kernel(geo, cot, fcol, w_in, b_in, w_mid, b_mid, w_head, out, g_in, g_mid, g_bin, g_bmid, g_head):
-    s = pl.program_id(0)
-    geo0, geo1 = geo[:, 0, :], geo[:, 1, :]
-    num, first = region_plan(geo0, s)
-    amount = jnp.sum(num).astype(jnp.int32)
+def backward_kernel(
+    chunks, geo, cot, rows_in, heads, w_mid, w_head, kept_in, out,
+    given, w_mid_half, head_half, g_in, g_mid, g_bin, g_bmid, g_head, kept, sem,
+):
+    geo0, cots_in = geo[:, 0, :], cot[...]
+    subs, enc, hid = g_in.shape
+    per = rows_in.shape[2] // 128
+    ends = []
+    total = jnp.int32(0)
+    for t in range(subs):
+        total = total + chunks[t]
+        ends.append(total)
+
+    def copy(slot, at):
+        return pltpu.make_async_copy(kept_in.at[at], kept.at[slot], sem.at[slot])
+
+    def fetch(n):
+        t, i = find(n, ends)
+        copy(n % 2, t * per + i).start()
+
+    @pl.when(total >= 1)
+    def _():
+        fetch(jnp.int32(0))
+
+    for t in range(subs):
+        src, place = region_map(*region_plan(geo0, t))
+        rows = region_take(cots_in, src, place, t)
+        w_mid_half[t] = w_mid[t] * 0.5
+        head_half[t] = (head_rows(w_head[t]) * 0.5).astype(BF16)
+        given[t] = jnp.concatenate(rows + rows, axis=0)
     for ref in (g_in, g_mid, g_bin, g_bmid, g_head):
         ref[...] = jnp.zeros_like(ref)
 
-    def step_of(i, carry):
-        src, place = chunk_map(num, first, i * CH)
-        head = chunk_take(geo0, src, place, s)
-        rest = chunk_take(geo1, src, place, s)
-        given = chunk_take(cot[...], src, place, s)
-        feat = encode(head, rest, fcol)
-        s1, h1, h1b, s2, h2, h2b = layers(feat, w_in[0], b_in[0], w_mid[0], b_mid[0])
-        head_t = lax.dot_general(w_head[0], h2b, NT, preferred_element_type=F32)[:8]
-        terms, passed = segment_terms(head_t, head[3], rest[3])
-        zero = jnp.zeros((1, 128), F32)
-        paint = jnp.concatenate([zero, given[0], given[1], given[2], zero, zero, zero, zero], axis=0)
+    def step_of(n, carry):
+        t, i = find(n, ends)
+        slot = n % 2
+
+        @pl.when(n + 1 < total)
+        def _():
+            fetch(n + 1)
+
+        lanes = pl.ds(pl.multiple_of(i * 128, 128), 128)
+        rows = rows_in[t, :, lanes]
+        cot_rows = given[t, :, lanes]
+        terms, passed = segment_terms(heads[t * per + i], rows[3:4, :], rows[7:8, :])
+        channel = iota((8, 128), 0)
+        paint = jnp.zeros((8, 128), F32)
+        for c in range(3):
+            paint = jnp.where(channel == c + 1, cot_rows[c : c + 1, :], paint)
         lower_half = iota((1, 128), 1) < CH
-        after = given[3] * passed
-        top_row = iota((8, 128), 0) == 0
+        after = cot_rows[3:4, :] * passed
+        top_row = channel == 0
         cots = [None] * 8
         for p in range(7, -1, -1):
             spacing, reach, keep, share, tint = terms[p]
@@ -300,32 +395,34 @@
             g_opt = (reach * keep * weight - later) * spacing
             cots[p] = jnp.where(top_row, g_opt * tint, paint * share * tint * (1.0 - tint))
         cot_t = jnp.concatenate(cots, axis=1)
-        cot_t = jnp.concatenate([cot_t, jnp.zeros_like(cot_t)], axis=0)
-        cot_b = cot_t.astype(BF16)
-        g_head[...] += jnp.dot(cot_b, h2b, preferred_element_type=F32)
-        gh2 = lax.dot_general(cot_b, w_head[0], TN, preferred_element_type=F32)
-        gz2 = gh2 * (s2 + h2 * (1.0 - s2))
+        cot_b = jnp.concatenate([cot_t, jnp.zeros_like(cot_t)], axis=0).astype(BF16)
+        copy(slot, 0).wait()
+        feat = kept[slot, :, 0:enc]
+        h1b = kept[slot, :, enc : enc + hid]
+        h2b = kept[slot, :, enc + hid : enc + 2 * hid]
+        slope1 = kept[slot, :, enc + 2 * hid : enc + 3 * hid].astype(F32)
+        slope2 = kept[slot, :, enc + 3 * hid : enc + 4 * hid].astype(F32)
+        g_head[t] += jnp.dot(cot_b, h2b, preferred_element_type=F32)
+        gz2 = lax.dot_general(cot_b, head_half[t], TN, preferred_element_type=F32) * slope2
         gz2b = gz2.astype(BF16)
-        g_mid[...] += lax.dot_general(h1b, gz2b, TN, preferred_element_type=F32)
-        g_bmid[...] += jnp.sum(gz2.reshape(-1, 8, gz2.shape[1]), axis=0)
-        gh1 = lax.dot_general(gz2b, w_mid[0], NT, preferred_element_type=F32)
-        gz1 = gh1 * (s1 + h1 * (1.0 - s1))
+        g_mid[t] += lax.dot_general(h1b, gz2b, TN, preferred_element_type=F32)
+        g_bmid[t] += jnp.sum(gz2.reshape(-1, 8, hid), axis=0)
+        gz1 = lax.dot_general(gz2b, w_mid_half[t], NT, preferred_element_type=F32) * slope1
         gz1b = gz1.astype(BF16)
-        g_in[...] += lax.dot_general(feat, gz1b, TN, preferred_element_type=F32)
-        g_bin[...] += jnp.sum(gz1.reshape(-1, 8, gz1.shape[1]), axis=0)
+        g_in[t] += lax.dot_general(feat, gz1b, TN, preferred_element_type=F32)
+        g_bin[t] += jnp.sum(gz1.reshape(-1, 8, hid), axis=0)
         return carry
 
-    lax.fori_loop(0, (amount + CH - 1) // CH, step_of, 0)
-    enc = g_in.shape[0]
-    hid = g_mid.shape[0]
-    out[0, 0:enc, :] = g_in[...].astype(BF16)
-    out[0, enc : enc + hid, :] = g_mid[...].astype(BF16)
-    row = iota(g_head.shape, 0)
-    b1 = jnp.sum(g_bin[...], axis=0, keepdims=True)
-    b2 = jnp.sum(g_bmid[...], axis=0, keepdims=True)
-    tail = jnp.where(row == 8, b1, jnp.where(row == 9, b2, g_head[...]))
-    out[0, enc + hid : enc + hid + 16, :] = tail.astype(BF16)
-    out[0, enc + hid + 16 : enc + hid + 32, :] = jnp.zeros_like(tail).astype(BF16)
+    lax.fori_loop(0, total, step_of, 0)
+    row = iota((16, hid), 0)
+    for t in range(subs):
+        out[t, 0:enc, :] = g_in[t].astype(BF16)
+        out[t, enc : enc + hid, :] = g_mid[t].astype(BF16)
+        b1 = jnp.sum(g_bin[t], axis=0, keepdims=True)
+        b2 = jnp.sum(g_bmid[t], axis=0, keepdims=True)
+        tail = jnp.where(row == 8, b1, jnp.where(row == 9, b2, g_head[t]))
+        out[t, enc + hid : enc + hid + 16, :] = tail.astype(BF16)
+        out[t, enc + hid + 16 :, :] = jnp.zeros((PAD - 16, hid), BF16)
 
 
 def total_kernel(parts, out):
@@ -371,13 +468,6 @@
     reps = lax.axis_size("rep")
     subs, enc, hid = w_input.shape
     rays = anchor.shape[1]
-    freqs = fourier.shape[1]
-    fcol = jnp.zeros((enc, 128), F32)
-    fcol = fcol.at[:, 0:3].set(jnp.concatenate([fourier.T, fourier.T], axis=0))
-    fcol = fcol.at[freqs:, 3].set(0.25)
-    w_head = jnp.pad(w_output, ((0, 0), (0, 12), (0, 0)))
-    b_in, b_mid = b_input[:, None, :], b_middle[:, None, :]
-
     geo_send, slot = call(
         send_kernel,
         (struct(groups, 2, 128), struct(1, rays * 4, dtype=jnp.int32)),
@@ -385,24 +475,23 @@
     )
     geo = a2a(geo_send, "region")
 
-    def whole(*shape):
-        return pl.BlockSpec(shape, lambda s: (0,) * len(shape))
-
-    def per_region(*shape):
-        return pl.BlockSpec((1,) + shape, lambda s: (s,) + (0,) * len(shape))
-
-    net_specs = [
-        whole(enc, 128), per_region(enc, hid), per_region(1, hid), per_region(hid, hid),
-        per_region(1, hid), per_region(16, hid),
-    ]
-    net = (fcol, w_input, b_in, w_middle, b_mid, w_head)
-    res = call(
+    wide = groups * 16
+    chunk_cap = subs * groups * 8 // CH
+    width = enc + 4 * hid
+    any_spec, vm_spec = pl.BlockSpec(memory_space=pl.ANY), pl.BlockSpec(memory_space=pltpu.VMEM)
+    sm_spec = pl.BlockSpec(memory_space=pltpu.SMEM)
+    res, seg_geo, heads, chunks, kept = call(
         forward_kernel,
-        struct(groups, 128),
-        geo, *net,
-        grid=(subs,),
-        in_specs=[whole(groups, 2, 128)] + net_specs,
-        out_specs=whole(groups, 128),
+        (
+            struct(groups, 128), struct(subs, 8, wide), struct(chunk_cap, 8, CH * SEG),
+            struct(subs, dtype=jnp.int32), struct(chunk_cap, CH * SEG, width, dtype=BF16),
+        ),
+        geo, fourier, w_input, b_input, w_middle, b_middle, w_output,
+        out_specs=(vm_spec, vm_spec, vm_spec, sm_spec, any_spec),
+        scratch_shapes=[
+            VM((subs, 8, wide), F32), VM((subs, enc, hid), BF16), VM((subs, hid, hid), BF16), VM((subs, 16, hid), BF16),
+            VM((2, CH * SEG, width), BF16), pltpu.SemaphoreType.DMA((2,)),
+        ],
     )
     res_back = a2a(res[:, None, :], "region")[:, 0, :]
     rendered, cot_send = call(
@@ -411,20 +500,20 @@
         slot, order.T, target, res_back,
     )
     cot = a2a(cot_send[:, None, :], "region")[:, 0, :]
-    rows = enc + hid + 32
+    rows = enc + hid + PAD
     packed = call(
         backward_kernel,
         struct(subs, rows, hid, dtype=BF16),
-        geo, cot, *net,
-        grid=(subs,),
-        in_specs=[whole(groups, 2, 128), whole(groups, 128)] + net_specs,
-        out_specs=per_region(rows, hid),
+        chunks, geo, cot, seg_geo, heads, w_middle, w_output, kept,
+        in_specs=[sm_spec] + [vm_spec] * 6 + [any_spec],
         scratch_shapes=[
-            VM((enc, hid), F32), VM((hid, hid), F32), VM((8, hid), F32), VM((8, hid), F32), VM((16, hid), F32),
+            VM((subs, 8, wide), F32), VM((subs, hid, hid), BF16), VM((subs, 16, hid), BF16),
+            VM((subs, enc, hid), F32), VM((subs, hid, hid), F32), VM((subs, 8, hid), F32), VM((subs, 8, hid), F32),
+            VM((subs, 16, hid), F32), VM((2, CH * SEG, width), BF16), pltpu.SemaphoreType.DMA((2,)),
         ],
     )
     parts = a2a(packed.reshape(reps, subs * rows // reps, hid), "rep")
-    mine = call(total_kernel, struct(subs * rows // reps, hid, dtype=BF16), parts)
+    mine = call(total_kernel, struct(*parts.shape[1:], dtype=BF16), parts)
     full = lax.all_gather(mine, "rep", axis=0, tiled=True).reshape(subs, rows, hid)
     grads = call(
         spread_kernel,

time: 165 us -> 149 us (0.903)
  Pallas kernels: 67.6 us -> 45.9 us
  blocking collectives: 81.3 us -> 102 us
  starting transfers between devices: 7.62 us -> 0 us
  local copies, waits for them, and re-layouts: 3.12 us -> 0 us
  waiting for transfers between devices: 2.24 us -> 0 us
    pallas_call x6, Pallas kernels: 67.6 us -> 45.9 us  [call(): pl.pallas_call(kernel, out_shape=outs, compiler_params=pltpu.CompilerPara...]
    all_to_all x3 -> x4, blocking collectives: 52.7 us -> 73.5 us  [a2a(): return lax.all_to_all(x, axis, split_axis=0, concat_axis=0, tiled=True)]
    all_to_all x1 -> x0, starting transfers between devices: 7.62 us -> none  [a2a(): return lax.all_to_all(x, axis, split_axis=0, concat_axis=0, tiled=True)]
    all_to_all x1 -> x0, waiting for transfers between devices: 2.24 us -> none  [a2a(): return lax.all_to_all(x, axis, split_axis=0, concat_axis=0, tiled=True)]
  transfers between devices with their start and end apart: 1 -> 0, of which waited for: 1 -> 0; matrix products, arithmetic and copies ran while one was open for 2% -> 0% of each run, Pallas kernels for 0% -> 0%
where the time goes in v1:
time: 149 us; the launch traced here: 148 us
  blocking collectives  102 us (68%)
  Pallas kernels  45.9 us (31%)
    all_to_all x4, blocking collectives, a2a(): return lax.all_to_all(x, axis, split_axis=0, concat_axis=0, tiled=True)  73.5 us
    pallas_call x6, Pallas kernels, call(): pl.pallas_call(kernel, out_shape=outs, compiler_params=pltpu.CompilerPara...  45.9 us
    all_gather x1, blocking collectives, body(): lax.all_gather(mine, 'rep', axis=0, tiled=True).reshape(subs, rows, hid)  28.2 us

profile of v1, /device:TPU:2, one launch (start us, length us, event | category | flops | bytes accessed | tf_op | source)
XLA Modules:
  0.0 148.3 jit_solution(12376466301563014796)
XLA Ops:
  0.6 2.0 %shard_map.181 = (f32[32,2,128]{2,1,0:T(2,128)}, s32[1,512]{1,0:T(1,128)}) custom-call(f32[3,128]{1,0:T(4,128)} %anchor.1, f32[3,128]{1,0:T(4,128)} %direction.1, f32[4,128]{1,0:T(4,128)} %start.1, bf16[4,128]{1,0:T(4,128)(2,1)} %step.1, s32[4,128]{1,0:T(4,128)} %counts.1, s32[4,128]{1,0:T(4,128)} %bitcast.18), custom_call_target="tpu_custom_call" | custom-call | tf_op jit(solution)/shard_map/pallas_call | solution.py:447
  2.7 13.9 %all_to_all.20.geo = f32[32,2,128]{2,1,0:T(2,128)} all-to-all(f32[32,2,128]{2,1,0:T(2,128)} %get-tuple-element.21), channel_id=1, replica_groups=mesh['rep'=8,'region'=32] {'region'}, dimensions={0} | all-to-all | bytes 65536 | tf_op jit(solution)/shard_map/all_to_all | solution.py:460
  16.6 20.0 %shard_map.182 = (f32[32,128]{1,0:T(8,128)}, f32[4,8,512]{2,1,0:T(8,128)}, f32[16,8,1024]{2,1,0:T(8,128)}, s32[4]{0:T(128)}, bf16[16,1024,1152]{2,1,0:T(8,128)(2,1)}) custom-call(f32[32,2,128]{2,1,0:T(2,128)} %all_to_all.20.geo, f32[3,64]{1,0:T(4,128)} %fourier.1, bf16[4,128,256]{2,1,0:T(8,128)(2,1)} %w_in.1, f32[4,256]{1,0:T(4,128)} %b_in.1, ...), custom_call_target="tpu_custom_call" | custom-call | tf_op jit(solution)/shard_map/pallas_call | solution.py:447
  36.6 13.6 %all_to_all.21 = f32[32,1,128]{2,1,0:T(1,128)} all-to-all(f32[32,1,128]{2,1,0:T(1,128)} %bitcast.16), channel_id=1, replica_groups=mesh['rep'=8,'region'=32] {'region'}, dimensions={0} | all-to-all | bytes 32768 | tf_op jit(solution)/shard_map/all_to_all | solution.py:460
  50.2 2.1 %shard_map.183 = (f32[3,128]{1,0:T(4,128)}, f32[32,128]{1,0:T(8,128)}) custom-call(s32[1,512]{1,0:T(1,128)} %get-tuple-element.20.slot, s32[4,128]{1,0:T(4,128)} %bitcast.19, f32[3,128]{1,0:T(4,128)} %target.1, f32[32,128]{1,0:T(8,128)} %bitcast.15), custom_call_target="tpu_custom_call" | custom-call | tf_op jit(solution)/shard_map/pallas_call | solution.py:447
  52.3 11.6 %all_to_all.22 = f32[32,1,128]{2,1,0:T(1,128)} all-to-all(f32[32,1,128]{2,1,0:T(1,128)} %bitcast.17), channel_id=1, replica_groups=mesh['rep'=8,'region'=32] {'region'}, dimensions={0} | all-to-all | bytes 32768 | tf_op jit(solution)/shard_map/all_to_all | solution.py:460
  63.9 17.5 %shard_map.184 = bf16[4,416,256]{2,1,0:T(8,128)(2,1)} custom-call(s32[4]{0:T(128)} %get-tuple-element.24.chunks, f32[32,2,128]{2,1,0:T(2,128)} %all_to_all.20.geo, f32[32,128]{1,0:T(8,128)} %bitcast.14, f32[4,8,512]{2,1,0:T(8,128)} %get-tuple-element.26.rows_in, f32[16,8,1024]{2,1,0:T(8,128)} %get-tuple-element.27.heads, bf16[4,256,256]{2,1,0:T(8,128)(2,1)} %w_mid.3, ...), custom_call_target="tpu_custom_call" | custom-call | tf_op jit(solution)/shard_map/pallas_call | solution.py:447
  81.4 34.4 %all_to_all.23.parts = bf16[8,208,256]{2,1,0:T(8,128)(2,1)} all-to-all(bf16[8,208,256]{2,1,0:T(8,128)(2,1)} %bitcast.13), channel_id=1, replica_groups=mesh['rep'=8,'region'=32] {'rep'}, dimensions={0} | all-to-all | bytes 1703936 | tf_op jit(solution)/shard_map/all_to_all | solution.py:460
  115.8 1.9 %shard_map.185 = bf16[208,256]{1,0:T(8,128)(2,1)} custom-call(bf16[8,208,256]{2,1,0:T(8,128)(2,1)} %all_to_all.23.parts), custom_call_target="tpu_custom_call" | custom-call | tf_op jit(solution)/shard_map/pallas_call | solution.py:447
  117.7 28.2 %all_gather.3 = bf16[1664,256]{1,0:T(8,128)(2,1)} all-gather(bf16[208,256]{1,0:T(8,128)(2,1)} %shard_map.185), channel_id=1, replica_groups=mesh['rep'=8,'region'=32] {'rep'}, dimensions={0}, use_global_device_ids=true | all-gather | bytes 958464 | tf_op jit(solution)/shard_map/all_gather | solution.py:517
  145.9 2.4 %shard_map.186 = (f32[4,128,256]{2,1,0:T(8,128)}, f32[4,256]{1,0:T(4,128)}, f32[4,256,256]{2,1,0:T(8,128)}, f32[4,256]{1,0:T(4,128)}, f32[4,4,256]{2,1,0:T(4,128)}) custom-call(bf16[4,416,256]{2,1,0:T(8,128)(2,1)} %bitcast.12), custom_call_target="tpu_custom_call" | custom-call | tf_op jit(solution)/shard_map/pallas_call | solution.py:447

commit v2 on v1

--- a/solution.py
+++ b/solution.py
@@ -10,6 +10,8 @@
 from jax.sharding import PartitionSpec as P
 
 SEG = 16
+BLOCK = 256
+BLOCKB = 512
 PAD = 32
 CH = 64
 F32, BF16 = jnp.float32, jnp.bfloat16
@@ -123,13 +125,19 @@
     return src.astype(BF16), place
 
 
-def region_take(arr, src, place, s):
-    full = pick(arr, src, TN, True)
+def region_take(arrs, src, place, s):
+    own = jnp.concatenate([a[w * 32 + s * 8 : w * 32 + s * 8 + 8, :] for a in arrs for w in range(4)], axis=0)
+    found = jnp.dot(jnp.concatenate(split3(own), axis=0), src, preferred_element_type=F32)
+    rows = own.shape[0]
+    full = (found[:rows] + found[rows : 2 * rows]) + found[2 * rows :]
     mask = iota((8, src.shape[1]), 0) == place
-    return [
-        jnp.sum(jnp.where(mask, full[w * 32 + s * 8 : w * 32 + s * 8 + 8, :], 0.0), axis=0, keepdims=True)
-        for w in range(4)
-    ]
+    return jnp.concatenate(
+        [
+            jnp.sum(jnp.where(mask, full[r : r + 8, :], 0.0), axis=0, keepdims=True)
+            for r in range(0, rows, 8)
+        ],
+        axis=0,
+    )
 
 
 def find(n, ends):
@@ -155,7 +163,7 @@
     for p in range(8):
         feats.append(sine_turns(begin).astype(BF16))
         begin = begin + slope
-    return jnp.concatenate(feats, axis=0)
+    return feats
 
 
 def columns_of(fourier):
@@ -213,6 +221,7 @@
     geo0, geo1 = geo[:, 0, :], geo[:, 1, :]
     enc, hid = w_in.shape[1:]
     subs = w_in.shape[0]
+    turned = (geo0.T, geo1.T)
     maps, ends = [], []
     total = jnp.int32(0)
     for s in range(subs):
@@ -226,9 +235,7 @@
         ends.append(total)
         src, place = region_map(num, first)
         maps.append((src, place))
-        rows_out[s] = jnp.concatenate(
-            region_take(geo0, src, place, s) + region_take(geo1, src, place, s), axis=0
-        )
+        rows_out[s] = region_take(turned, src, place, s)
     seg_rows[...] = jnp.zeros_like(seg_rows)
     per = rows_out.shape[2] // 128
 
@@ -246,13 +253,20 @@
         lanes = pl.ds(pl.multiple_of(i * 128, 128), 128)
         rows = rows_out[s, :, lanes]
         rows = [rows[w : w + 1, :] for w in range(8)]
-        feat = encode(rows[:4], rows[4:], fcol)
-        h1b, slope1 = layer(feat, w_in_half[s], b_in[pl.ds(s, 1), :] * 0.5)
-        h2b, slope2 = layer(h1b, w_mid_half[s], b_mid[pl.ds(s, 1), :] * 0.5)
-        at = 0
-        for part in (feat, h1b, h2b, slope1, slope2):
-            kept[slot, :, at : at + part.shape[1]] = part
-            at += part.shape[1]
+        feats = encode(rows[:4], rows[4:], fcol)
+        w1, w2 = w_in_half[s], w_mid_half[s]
+        b1, b2 = b_in[pl.ds(s, 1), :] * 0.5, b_mid[pl.ds(s, 1), :] * 0.5
+        h2_blocks = []
+        for q in range(0, CH * SEG, BLOCK):
+            feat = jnp.concatenate(feats[q // 128 : (q + BLOCK) // 128], axis=0)
+            h1b, slope1 = layer(feat, w1, b1)
+            h2b, slope2 = layer(h1b, w2, b2)
+            at = 0
+            for part in (feat, h1b, h2b, slope1, slope2):
+                kept[slot, q : q + BLOCK, at : at + part.shape[1]] = part
+                at += part.shape[1]
+            h2_blocks.append(h2b)
+        h2b = jnp.concatenate(h2_blocks, axis=0)
         copy(slot, s * per + i).start()
         head_t = lax.dot_general(heads[s], h2b, NT, preferred_element_type=F32)[:8]
         heads_out[s * per + i] = head_t
@@ -274,19 +288,19 @@
     def _():
         copy(total % 2, 0).wait()
 
-    acc = jnp.zeros(res_out.shape, F32)
+    found = []
     for s in range(subs):
         src, place = maps[s]
         wide = src.shape[1]
         mask = (iota((8, wide), 0) == place) & (iota((8, wide), 1) % 128 < CH)
-        none = jnp.zeros((8, wide), F32)
-        blocks = []
-        for w in range(4):
-            row = (w + 1) % 4
-            hit = jnp.where(mask, seg_rows[s, row : row + 1, :], 0.0)
-            blocks += [hit if t == s else none for t in range(4)]
-        acc = acc + pick(src, jnp.concatenate(blocks, axis=0), NT, False)
-    res_out[...] = acc
+        own = jnp.concatenate(
+            [jnp.where(mask, seg_rows[s, r : r + 1, :], 0.0) for r in (1, 2, 3, 0)], axis=0
+        )
+        full = lax.dot_general(jnp.concatenate(split3(own), axis=0), src, NT, preferred_element_type=F32)
+        found.append((full[0:32] + full[32:64]) + full[64:96])
+    res_out[...] = jnp.concatenate(
+        [found[s][w * 8 : w * 8 + 8, :] for w in range(4) for s in range(subs)], axis=0
+    ).T
 
 
 def merge_kernel(slot, order, target, res, rendered_out, cot_out):
@@ -336,7 +350,7 @@
     chunks, geo, cot, rows_in, heads, w_mid, w_head, kept_in, out,
     given, w_mid_half, head_half, g_in, g_mid, g_bin, g_bmid, g_head, kept, sem,
 ):
-    geo0, cots_in = geo[:, 0, :], cot[...]
+    geo0, turned = geo[:, 0, :], cot[...].T
     subs, enc, hid = g_in.shape
     per = rows_in.shape[2] // 128
     ends = []
@@ -358,10 +372,10 @@
 
     for t in range(subs):
         src, place = region_map(*region_plan(geo0, t))
-        rows = region_take(cots_in, src, place, t)
+        rows = region_take((turned,), src, place, t)
         w_mid_half[t] = w_mid[t] * 0.5
         head_half[t] = (head_rows(w_head[t]) * 0.5).astype(BF16)
-        given[t] = jnp.concatenate(rows + rows, axis=0)
+        given[t] = jnp.concatenate([rows, rows], axis=0)
     for ref in (g_in, g_mid, g_bin, g_bmid, g_head):
         ref[...] = jnp.zeros_like(ref)
 
@@ -400,17 +414,25 @@
         feat = kept[slot, :, 0:enc]
         h1b = kept[slot, :, enc : enc + hid]
         h2b = kept[slot, :, enc + hid : enc + 2 * hid]
-        slope1 = kept[slot, :, enc + 2 * hid : enc + 3 * hid].astype(F32)
-        slope2 = kept[slot, :, enc + 3 * hid : enc + 4 * hid].astype(F32)
         g_head[t] += jnp.dot(cot_b, h2b, preferred_element_type=F32)
-        gz2 = lax.dot_general(cot_b, head_half[t], TN, preferred_element_type=F32) * slope2
-        gz2b = gz2.astype(BF16)
+        cot_rows_b = cot_b.astype(F32).T.astype(BF16)
+        gz2_blocks, gz1_blocks = [], []
+        sum1 = sum2 = jnp.zeros((8, hid), F32)
+        for q in range(0, CH * SEG, BLOCKB):
+            slope2 = kept[slot, q : q + BLOCKB, enc + 3 * hid : enc + 4 * hid].astype(F32)
+            gz2 = jnp.dot(cot_rows_b[q : q + BLOCKB], head_half[t], preferred_element_type=F32) * slope2
+            gz2b = gz2.astype(BF16)
+            sum2 = sum2 + jnp.sum(gz2.reshape(-1, 8, hid), axis=0)
+            slope1 = kept[slot, q : q + BLOCKB, enc + 2 * hid : enc + 3 * hid].astype(F32)
+            gz1 = lax.dot_general(gz2b, w_mid_half[t], NT, preferred_element_type=F32) * slope1
+            sum1 = sum1 + jnp.sum(gz1.reshape(-1, 8, hid), axis=0)
+            gz2_blocks.append(gz2b)
+            gz1_blocks.append(gz1.astype(BF16))
+        gz2b, gz1b = jnp.concatenate(gz2_blocks, axis=0), jnp.concatenate(gz1_blocks, axis=0)
         g_mid[t] += lax.dot_general(h1b, gz2b, TN, preferred_element_type=F32)
-        g_bmid[t] += jnp.sum(gz2.reshape(-1, 8, hid), axis=0)
-        gz1 = lax.dot_general(gz2b, w_mid_half[t], NT, preferred_element_type=F32) * slope1
-        gz1b = gz1.astype(BF16)
+        g_bmid[t] += sum2
+        g_bin[t] += sum1
         g_in[t] += lax.dot_general(feat, gz1b, TN, preferred_element_type=F32)
-        g_bin[t] += jnp.sum(gz1.reshape(-1, 8, hid), axis=0)
         return carry
 
     lax.fori_loop(0, total, step_of, 0)

time: 149 us -> 150 us (level); the launches traced: 148 us -> 147 us
  Pallas kernels: 45.9 us -> 38.8 us
  blocking collectives: 102 us -> 107 us
    pallas_call x6, Pallas kernels: 45.9 us -> 38.8 us  [call(): pl.pallas_call(kernel, out_shape=outs, compiler_params=pltpu.CompilerPara...]
    all_to_all x4, blocking collectives: 73.5 us -> 78.8 us  [a2a(): return lax.all_to_all(x, axis, split_axis=0, concat_axis=0, tiled=True)]
where the time goes in v2:
time: 150 us; the launch traced here: 147 us
  blocking collectives  107 us (71%)
  Pallas kernels  38.8 us (26%)
    all_to_all x4, blocking collectives, a2a(): return lax.all_to_all(x, axis, split_axis=0, concat_axis=0, tiled=True)  78.8 us
    pallas_call x6, Pallas kernels, call(): pl.pallas_call(kernel, out_shape=outs, compiler_params=pltpu.CompilerPara...  38.8 us
    all_gather x1, blocking collectives, body(): lax.all_gather(mine, 'rep', axis=0, tiled=True).reshape(subs, rows, hid)  28.4 us

profile of v2, /device:TPU:2, one launch (start us, length us, event | category | flops | bytes accessed | tf_op | source)
XLA Modules:
  0.0 146.7 jit_solution(15053308044494998623)
XLA Ops:
  0.6 2.0 %shard_map.181 = (f32[32,2,128]{2,1,0:T(2,128)}, s32[1,512]{1,0:T(1,128)}) custom-call(f32[3,128]{1,0:T(4,128)} %anchor.1, f32[3,128]{1,0:T(4,128)} %direction.1, f32[4,128]{1,0:T(4,128)} %start.1, bf16[4,128]{1,0:T(4,128)(2,1)} %step.1, s32[4,128]{1,0:T(4,128)} %counts.1, s32[4,128]{1,0:T(4,128)} %bitcast.18), custom_call_target="tpu_custom_call" | custom-call | tf_op jit(solution)/shard_map/pallas_call | solution.py:469
  2.7 13.9 %all_to_all.20.geo = f32[32,2,128]{2,1,0:T(2,128)} all-to-all(f32[32,2,128]{2,1,0:T(2,128)} %get-tuple-element.21), channel_id=1, replica_groups=mesh['rep'=8,'region'=32] {'region'}, dimensions={0} | all-to-all | bytes 65536 | tf_op jit(solution)/shard_map/all_to_all | solution.py:482
  16.6 16.3 %shard_map.182 = (f32[32,128]{1,0:T(8,128)}, f32[4,8,512]{2,1,0:T(8,128)}, f32[16,8,1024]{2,1,0:T(8,128)}, s32[4]{0:T(128)}, bf16[16,1024,1152]{2,1,0:T(8,128)(2,1)}) custom-call(f32[32,2,128]{2,1,0:T(2,128)} %all_to_all.20.geo, f32[3,64]{1,0:T(4,128)} %fourier.1, bf16[4,128,256]{2,1,0:T(8,128)(2,1)} %w_in.1, f32[4,256]{1,0:T(4,128)} %b_in.1, ...), custom_call_target="tpu_custom_call" | custom-call | tf_op jit(solution)/shard_map/pallas_call | solution.py:469
  32.9 17.3 %all_to_all.21 = f32[32,1,128]{2,1,0:T(1,128)} all-to-all(f32[32,1,128]{2,1,0:T(1,128)} %bitcast.16), channel_id=1, replica_groups=mesh['rep'=8,'region'=32] {'region'}, dimensions={0} | all-to-all | bytes 32768 | tf_op jit(solution)/shard_map/all_to_all | solution.py:482
  50.2 2.1 %shard_map.183 = (f32[3,128]{1,0:T(4,128)}, f32[32,128]{1,0:T(8,128)}) custom-call(s32[1,512]{1,0:T(1,128)} %get-tuple-element.20.slot, s32[4,128]{1,0:T(4,128)} %bitcast.19, f32[3,128]{1,0:T(4,128)} %target.1, f32[32,128]{1,0:T(8,128)} %bitcast.15), custom_call_target="tpu_custom_call" | custom-call | tf_op jit(solution)/shard_map/pallas_call | solution.py:469
  52.3 11.6 %all_to_all.22 = f32[32,1,128]{2,1,0:T(1,128)} all-to-all(f32[32,1,128]{2,1,0:T(1,128)} %bitcast.17), channel_id=1, replica_groups=mesh['rep'=8,'region'=32] {'region'}, dimensions={0} | all-to-all | bytes 32768 | tf_op jit(solution)/shard_map/all_to_all | solution.py:482
  63.9 14.1 %shard_map.184 = bf16[4,416,256]{2,1,0:T(8,128)(2,1)} custom-call(s32[4]{0:T(128)} %get-tuple-element.24.chunks, f32[32,2,128]{2,1,0:T(2,128)} %all_to_all.20.geo, f32[32,128]{1,0:T(8,128)} %bitcast.14, f32[4,8,512]{2,1,0:T(8,128)} %get-tuple-element.26.rows_in, f32[16,8,1024]{2,1,0:T(8,128)} %get-tuple-element.27.heads, bf16[4,256,256]{2,1,0:T(8,128)(2,1)} %w_mid.3, ...), custom_call_target="tpu_custom_call" | custom-call | tf_op jit(solution)/shard_map/pallas_call | solution.py:469
  78.1 35.9 %all_to_all.23.parts = bf16[8,208,256]{2,1,0:T(8,128)(2,1)} all-to-all(bf16[8,208,256]{2,1,0:T(8,128)(2,1)} %bitcast.13), channel_id=1, replica_groups=mesh['rep'=8,'region'=32] {'rep'}, dimensions={0} | all-to-all | bytes 1703936 | tf_op jit(solution)/shard_map/all_to_all | solution.py:482
  114.0 1.9 %shard_map.185 = bf16[208,256]{1,0:T(8,128)(2,1)} custom-call(bf16[8,208,256]{2,1,0:T(8,128)(2,1)} %all_to_all.23.parts), custom_call_target="tpu_custom_call" | custom-call | tf_op jit(solution)/shard_map/pallas_call | solution.py:469
  115.9 28.4 %all_gather.3 = bf16[1664,256]{1,0:T(8,128)(2,1)} all-gather(bf16[208,256]{1,0:T(8,128)(2,1)} %shard_map.185), channel_id=1, replica_groups=mesh['rep'=8,'region'=32] {'rep'}, dimensions={0}, use_global_device_ids=true | all-gather | bytes 958464 | tf_op jit(solution)/shard_map/all_gather | solution.py:539
  144.4 2.4 %shard_map.186 = (f32[4,128,256]{2,1,0:T(8,128)}, f32[4,256]{1,0:T(4,128)}, f32[4,256,256]{2,1,0:T(8,128)}, f32[4,256]{1,0:T(4,128)}, f32[4,4,256]{2,1,0:T(4,128)}) custom-call(bf16[4,416,256]{2,1,0:T(8,128)(2,1)} %bitcast.12), custom_call_target="tpu_custom_call" | custom-call | tf_op jit(solution)/shard_map/pallas_call | solution.py:469

commit v3 on v2

--- a/solution.py
+++ b/solution.py
@@ -536,7 +536,11 @@
     )
     parts = a2a(packed.reshape(reps, subs * rows // reps, hid), "rep")
     mine = call(total_kernel, struct(*parts.shape[1:], dtype=BF16), parts)
-    full = lax.all_gather(mine, "rep", axis=0, tiled=True).reshape(subs, rows, hid)
+    pairs = [[r, r + 1] for r in range(0, reps, 2)]
+    strides = [list(range(k, reps, 2)) for k in range(2)]
+    for members in (pairs, strides):
+        mine = lax.all_gather(mine, "rep", axis=0, tiled=True, axis_index_groups=members)
+    full = mine.reshape(subs, rows, hid)
     grads = call(
         spread_kernel,
         (struct(subs, enc, hid), struct(subs, hid), struct(subs, hid, hid), struct(subs, hid), struct(subs, 4, hid)),

time: 150 us -> 147 us (0.980)
  blocking collectives: 107 us -> 103 us
  Pallas kernels: 38.8 us -> 41.6 us
    all_gather x1 -> x2, blocking collectives: 28.4 us -> 25.2 us  [body(): lax.all_gather(mine, 'rep', axis=0, tiled=True, axis_index_groups=members)]
    pallas_call x6, Pallas kernels: 38.8 us -> 41.6 us  [call(): pl.pallas_call(kernel, out_shape=outs, compiler_params=pltpu.CompilerPara...]
where the time goes in v3:
time: 147 us; the launch traced here: 145 us
  blocking collectives  103 us (70%)
  Pallas kernels  41.6 us (28%)
    all_to_all x4, blocking collectives, a2a(): return lax.all_to_all(x, axis, split_axis=0, concat_axis=0, tiled=True)  77.5 us
    pallas_call x6, Pallas kernels, call(): pl.pallas_call(kernel, out_shape=outs, compiler_params=pltpu.CompilerPara...  41.6 us
    all_gather x2, blocking collectives, body(): lax.all_gather(mine, 'rep', axis=0, tiled=True, axis_index_groups=members)  25.2 us

profile of v3, /device:TPU:2, one launch (start us, length us, event | category | flops | bytes accessed | tf_op | source)
XLA Modules:
  0.0 144.9 jit_solution(2571776840081291607)
XLA Ops:
  0.6 2.0 %shard_map.181 = (f32[32,2,128]{2,1,0:T(2,128)}, s32[1,512]{1,0:T(1,128)}) custom-call(f32[3,128]{1,0:T(4,128)} %anchor.1, f32[3,128]{1,0:T(4,128)} %direction.1, f32[4,128]{1,0:T(4,128)} %start.1, bf16[4,128]{1,0:T(4,128)(2,1)} %step.1, s32[4,128]{1,0:T(4,128)} %counts.1, s32[4,128]{1,0:T(4,128)} %bitcast.18), custom_call_target="tpu_custom_call" | custom-call | tf_op jit(solution)/shard_map/pallas_call | solution.py:469
  2.7 13.9 %all_to_all.20.geo = f32[32,2,128]{2,1,0:T(2,128)} all-to-all(f32[32,2,128]{2,1,0:T(2,128)} %get-tuple-element.21), channel_id=1, replica_groups=mesh['rep'=8,'region'=32] {'region'}, dimensions={0} | all-to-all | bytes 65536 | tf_op jit(solution)/shard_map/all_to_all | solution.py:482
  16.6 17.7 %shard_map.182 = (f32[32,128]{1,0:T(8,128)}, f32[4,8,512]{2,1,0:T(8,128)}, f32[16,8,1024]{2,1,0:T(8,128)}, s32[4]{0:T(128)}, bf16[16,1024,1152]{2,1,0:T(8,128)(2,1)}) custom-call(f32[32,2,128]{2,1,0:T(2,128)} %all_to_all.20.geo, f32[3,64]{1,0:T(4,128)} %fourier.1, bf16[4,128,256]{2,1,0:T(8,128)(2,1)} %w_in.1, f32[4,256]{1,0:T(4,128)} %b_in.1, ...), custom_call_target="tpu_custom_call" | custom-call | tf_op jit(solution)/shard_map/pallas_call | solution.py:469
  34.3 17.3 %all_to_all.21 = f32[32,1,128]{2,1,0:T(1,128)} all-to-all(f32[32,1,128]{2,1,0:T(1,128)} %bitcast.16), channel_id=1, replica_groups=mesh['rep'=8,'region'=32] {'region'}, dimensions={0} | all-to-all | bytes 32768 | tf_op jit(solution)/shard_map/all_to_all | solution.py:482
  51.7 2.1 %shard_map.183 = (f32[3,128]{1,0:T(4,128)}, f32[32,128]{1,0:T(8,128)}) custom-call(s32[1,512]{1,0:T(1,128)} %get-tuple-element.20.slot, s32[4,128]{1,0:T(4,128)} %bitcast.19, f32[3,128]{1,0:T(4,128)} %target.1, f32[32,128]{1,0:T(8,128)} %bitcast.15), custom_call_target="tpu_custom_call" | custom-call | tf_op jit(solution)/shard_map/pallas_call | solution.py:469
  53.7 11.6 %all_to_all.22 = f32[32,1,128]{2,1,0:T(1,128)} all-to-all(f32[32,1,128]{2,1,0:T(1,128)} %bitcast.17), channel_id=1, replica_groups=mesh['rep'=8,'region'=32] {'region'}, dimensions={0} | all-to-all | bytes 32768 | tf_op jit(solution)/shard_map/all_to_all | solution.py:482
  65.3 15.4 %shard_map.184 = bf16[4,416,256]{2,1,0:T(8,128)(2,1)} custom-call(s32[4]{0:T(128)} %get-tuple-element.24.chunks, f32[32,2,128]{2,1,0:T(2,128)} %all_to_all.20.geo, f32[32,128]{1,0:T(8,128)} %bitcast.14, f32[4,8,512]{2,1,0:T(8,128)} %get-tuple-element.26.rows_in, f32[16,8,1024]{2,1,0:T(8,128)} %get-tuple-element.27.heads, bf16[4,256,256]{2,1,0:T(8,128)(2,1)} %w_mid.3, ...), custom_call_target="tpu_custom_call" | custom-call | tf_op jit(solution)/shard_map/pallas_call | solution.py:469
  80.8 34.6 %all_to_all.23.parts = bf16[8,208,256]{2,1,0:T(8,128)(2,1)} all-to-all(bf16[8,208,256]{2,1,0:T(8,128)(2,1)} %bitcast.13), channel_id=1, replica_groups=mesh['rep'=8,'region'=32] {'rep'}, dimensions={0} | all-to-all | bytes 1703936 | tf_op jit(solution)/shard_map/all_to_all | solution.py:482
  115.4 1.9 %shard_map.185 = bf16[208,256]{1,0:T(8,128)(2,1)} custom-call(bf16[8,208,256]{2,1,0:T(8,128)(2,1)} %all_to_all.23.parts), custom_call_target="tpu_custom_call" | custom-call | tf_op jit(solution)/shard_map/pallas_call | solution.py:469
  117.3 5.6 %all_gather.6 = bf16[416,256]{1,0:T(8,128)(2,1)S(1)} all-gather(bf16[208,256]{1,0:T(8,128)(2,1)} %shard_map.185), channel_id=1, replica_groups={{0,32},{64,96},{128,160},{192,224},{1,33},{65,97},{129,161},{193,225},{..., dimensions={0}, use_global_device_ids=true | all-gather | bytes 319488 | tf_op jit(solution)/shard_map/all_gather | solution.py:542
  122.9 19.6 %all_gather.7 = bf16[1664,256]{1,0:T(8,128)(2,1)} all-gather(bf16[416,256]{1,0:T(8,128)(2,1)S(1)} %all_gather.6), channel_id=1, replica_groups={{0,64,128,192},{32,96,160,224},{1,65,129,193},{33,97,161,225},{2,66,130..., dimensions={0}, use_global_device_ids=true | all-gather | bytes 1064960 | tf_op jit(solution)/shard_map/all_gather | solution.py:542
  142.5 2.4 %shard_map.186 = (f32[4,128,256]{2,1,0:T(8,128)}, f32[4,256]{1,0:T(4,128)}, f32[4,256,256]{2,1,0:T(8,128)}, f32[4,256]{1,0:T(4,128)}, f32[4,4,256]{2,1,0:T(4,128)}) custom-call(bf16[4,416,256]{2,1,0:T(8,128)(2,1)} %bitcast.12), custom_call_target="tpu_custom_call" | custom-call | tf_op jit(solution)/shard_map/pallas_call | solution.py:469
